TPU v7x, 128 devices: a whole 4x4x4 slice. The times are simulated.
128 devices in a mesh: grp: 4 (over x), dev: 32 (over z, y, core).
Axes of the slice: x: 4, y: 4, z: 4, core: 2. Of those that a mesh axis runs over, the one named last changes fastest.
Arguments:
- flat_master: float32 [9728, 128, 128], P(('grp', 'dev')), may hold values from -2 to 2
- norm_gains: float32 [2048], P(('grp', 'dev')), may hold values from 0.1 to 1.9
- place: int32 [128, 76], replicated, may hold values from 0 to 9727, as said below
- serve_rank: int32 [128], replicated, may hold values from 0 to 127, each once
Outputs:
- qk_absorbed: bfloat16 [128, 1536, 512], P(('grp', 'dev'))
- vo_absorbed: bfloat16 [128, 512, 7168], P(('grp', 'dev'))
Inputs may be any that keep to these rules, and one draw needn't show every extreme that they name: place is a permutation of all flat block indices; flat block index b lies on device b // 76; each device holds at most 1 block of any one head, so its 76 blocks belong to 76 distinct heads.
All inputs are finite; a program needn't handle non-finite values.
Results may differ from a plain program's by a relative error of at most 0.001.
Values sent between devices are 32-bit elements; how exact they have to be, the bound alone decides.
A program may use at most 128 MiB of HBM per device.

v0:
```python
import jax
import jax.numpy as jnp
from jax import lax
from jax.sharding import PartitionSpec as P

QL = 1536
KL = 512
D = 7168


def absorb(blocks, gain_q, gain_kv, head_size, q_width, kv_width, model_width):
    qb = q_width // head_size
    kb = kv_width // head_size
    w_uq = blocks[:qb].reshape(q_width, head_size)
    w_uk = blocks[qb : qb + kb].reshape(kv_width, head_size)
    w_uv = blocks[qb + kb : qb + 2 * kb].reshape(kv_width, head_size)
    w_out = blocks[qb + 2 * kb :].transpose(1, 0, 2).reshape(head_size, model_width)
    query_key = jnp.dot(
        w_uq, w_uk.T, precision=lax.Precision.HIGHEST, preferred_element_type=jnp.float32
    )
    query_key = query_key * gain_q[:, None] * gain_kv[None, :]
    value_out = jnp.dot(
        w_uv, w_out, precision=lax.Precision.HIGHEST, preferred_element_type=jnp.float32
    )
    value_out = value_out * gain_kv[:, None]
    return (query_key.astype(jnp.bfloat16), value_out.astype(jnp.bfloat16))


def body(flat_master, norm_gains, place, serve_rank):
    groups = lax.axis_size("grp")
    members = lax.axis_size("dev")
    devcount = groups * members
    myself = lax.axis_index("grp") * members + lax.axis_index("dev")
    nblocks = flat_master.shape[0]
    head_size = flat_master.shape[1]
    capacity = (nblocks + devcount - 1) // devcount
    heads = place.shape[0]
    holder = place // nblocks
    mine = (holder == myself).astype(jnp.int32)
    earlier = jnp.cumsum(mine, axis=1) - mine
    target_row = serve_rank[:, None] * capacity + earlier
    local = place % nblocks
    match = (mine[:, :, None] == 1) & (
        local[:, :, None] == jnp.arange(nblocks, dtype=jnp.int32)[None, None, :]
    )
    target = jnp.sum(jnp.where(match, target_row[:, :, None], 0), axis=(0, 1))
    outgoing = (
        jnp.zeros((devcount * capacity, head_size, head_size), jnp.float32)
        .at[target]
        .set(flat_master)
    )
    arrived = lax.all_to_all(
        outgoing.reshape(devcount, capacity, head_size, head_size),
        ("grp", "dev"),
        split_axis=0,
        concat_axis=0,
        tiled=True,
    )
    arrived = arrived.reshape(devcount * capacity, head_size, head_size)
    gains_all = lax.all_gather(norm_gains, ("grp", "dev"), axis=0, tiled=True)
    q_width = QL
    kv_width = KL
    gain_q = gains_all[:q_width]
    gain_kv = gains_all[q_width : q_width + kv_width]
    served = jnp.sum(jnp.where(serve_rank == myself, jnp.arange(heads, dtype=jnp.int32), 0))
    head_rows = lax.dynamic_index_in_dim(place, served, 0, keepdims=False)
    source = head_rows // nblocks
    order = jnp.arange(nblocks, dtype=jnp.int32)
    same_source = (source[:, None] == source[None, :]) & (order[None, :] < order[:, None])
    position = jnp.sum(same_source.astype(jnp.int32), axis=1)
    blocks = arrived[source * capacity + position]
    query_key, value_out = absorb(blocks, gain_q, gain_kv, head_size, q_width, kv_width, D)
    return (query_key[None], value_out[None])


def solution(mesh):
    in_specs = (P(("grp", "dev"), None, None), P(("grp", "dev")), P(), P())
    out_specs = (P(("grp", "dev"), None, None), P(("grp", "dev"), None, None))
    return jax.shard_map(body, mesh=mesh, in_specs=in_specs, out_specs=out_specs, check_vma=False)
```

profile of v0, /device:TPU:1, one launch (start us, length us, event | category | flops | bytes accessed | tf_op | source)
XLA Modules:
  0.0 233.0 jit_solution(7690065545811122550)
XLA Ops:
  0.6 0.8 broadcast_compare_fusion
  1.5 0.1 reduce_window_sum.11
  1.6 0.8 add_select_fusion.1
  2.4 1.1 select_reduce_fusion
  3.5 4.3 %broadcast_in_dim.22 = f32[128,128,128]{2,1,0:T(8,128)} broadcast(f32[]{:T(128)} %constant.40.clone.1), dimensions={} | broadcast | bytes 8388612 | tf_op jit(solution)/shard_map/broadcast_in_dim | solution.py:48
  7.8 14.7 %scatter_fusion = f32[128,128,128]{2,1,0:T(8,128)} fusion(f32[128,128,128]{2,1,0:T(8,128)} %broadcast_in_dim.22, s32[76]{0:T(128)S(1)} %fusion.14, f32[76,128,128]{2,1,0:T(8,128)} %param.4), kind=kCustom, calls=%fused_computation.1 | custom fusion | bytes 14942512 | tf_op jit(solution)/shard_map/scatter | solution.py:50
  22.5 0.0 copy-start.1
  22.5 0.0 copy-start.2
  22.5 0.0 copy-start
  22.5 11.9 %all-to-all-start = ((f32[128,1,128,128]{3,2,1,0:T(8,128)}), f32[128,1,128,128]{3,2,1,0:T(8,128)}, u32[]{:S(2)}, u32[]{:S(2)}) async-start(f32[128,1,128,128]{3,2,1,0:T(8,128)} %bitcast.39), calls=%async_computation | async-start | bytes 16777216 | tf_op jit(solution)/shard_map/all_to_all | solution.py:52
  34.4 0.0 copy-done.1
  34.4 0.6 fusion.12
  36.3 0.0 copy-done.2
  36.4 0.3 dynamic-update-slice
  36.6 158.6 %all-reduce = f32[2048]{0:T(1024)S(1)} all-reduce(f32[2048]{0:T(1024)S(1)} %dynamic-update-slice), channel_id=1, replica_groups=mesh['grp'=4,'dev'=32] {'grp','dev'}, use_global_device_ids=true, to_apply=%add | all-reduce | flops 2048 | bytes 16384
  195.9 0.0 copy-done
  196.0 0.2 fusion.16
  196.1 0.2 fusion.11
  196.4 0.2 convert_reduce_fusion
  196.6 0.0 all-to-all-done
  196.6 6.5 %gather_fusion = f32[76,128,128]{2,1,0:T(8,128)} fusion(f32[128,128,128]{2,1,0:T(8,128)} %bitcast.4, s32[1024]{0:T(1024)S(1)} %pad_clamp_fusion), kind=kCustom, calls=%fused_computation | custom fusion | bytes 9961776 | tf_op jit(solution)/shard_map/gather | solution.py:71
  203.1 1.1 fusion.19
  204.2 4.3 %slice_bitcast_fusion = f32[128,56,128]{2,0,1:T(8,128)} fusion(f32[76,128,128]{2,1,0:T(8,128)} %gather_fusion), kind=kLoop, calls=%fused_computation.4 | loop fusion | bytes 7340032 | tf_op jit(solution)/shard_map/transpose | solution.py:17
  208.5 5.3 %copy.23 = f32[128,56,128]{0,2,1:T(8,128)} copy(f32[128,56,128]{2,0,1:T(8,128)} %slice_bitcast_fusion) | data formatting | bytes 7340032 | tf_op jit(solution)/shard_map/transpose | solution.py:17
  213.7 0.0 slice-start
  213.7 15.4 %fusion = bf16[1,512,7168]{2,1,0:T(8,128)(2,1)} fusion(f32[512,128]{1,0:T(8,128)S(1)} %bitcast.42, f32[128,7168]{0,1:T(8,128)} %bitcast.41, f32[512]{0:T(512)S(1)} %slice.29), kind=kOutput, calls=%fused_computation.3 | convolution fusion | flops 5644484608 | bytes 11274240 | tf_op jit(solution)/shard_map/dot_general | solution.py:22
  229.1 0.0 slice-done
  229.1 3.9 %fusion.4 = bf16[1,1536,512]{2,1,0:T(8,128)(2,1)} fusion(f32[1536,128]{1,0:T(8,128)S(1)} %bitcast.40, f32[512,128]{1,0:T(8,128)S(1)} %bitcast.43, f32[512]{0:T(512)S(1)} %slice.29, f32[1536]{0:T(1024)S(1)} %bitcast.44), kind=kOutput, calls=%fused_computation.11 | convolution fusion | flops 1210318848 | bytes 2629632 | tf_op jit(solution)/shard_map/dot_general | solution.py:18
  (6 shorter events, 0.0 us)
Async XLA Ops:
  22.5 11.9 %copy-start.1 = (s32[128]{0:T(128)S(1)}, s32[128]{0:T(128)}, u32[]{:S(2)}) copy-start(s32[128]{0:T(128)} %param.7) | copy-start | bytes 1540
  22.5 13.9 %copy-start.2 = (f32[16]{0:T(128)S(1)}, f32[16]{0:T(128)}, u32[]{:S(2)}) copy-start(f32[16]{0:T(128)} %param.5) | copy-start | bytes 196
  22.5 173.5 %copy-start = (s32[128,76]{0,1:T(8,128)S(1)}, s32[128,76]{0,1:T(8,128)}, u32[]{:S(2)}) copy-start(s32[128,76]{0,1:T(8,128)} %param.6) | copy-start | bytes 116740
  22.5 174.1 %all-to-all-start = ((f32[128,1,128,128]{3,2,1,0:T(8,128)}), f32[128,1,128,128]{3,2,1,0:T(8,128)}, u32[]{:S(2)}, u32[]{:S(2)}) async-start(f32[128,1,128,128]{3,2,1,0:T(8,128)} %bitcast.39), calls=%async_computation | async-start | bytes 16777216 | tf_op jit(solution)/shard_map/all_to_all | solution.py:52
  213.7 15.4 %slice-start = ((f32[76,128,128]{2,1,0:T(8,128)}), f32[12,128,128]{2,1,0:T(8,128)S(1)}, s32[]{:S(2)}) async-start(f32[76,128,128]{2,1,0:T(8,128)} %gather_fusion), calls=%async_computation.1 | async-start | bytes 1572864 | tf_op jit(solution)/shard_map/slice | solution.py:14
where the time goes:
time: 234 us; the launch traced here: 233 us
  blocking collectives  159 us (68%)
  local copies, waits for them, and re-layouts  36.4 us (16%)
  matrix products  19.2 us (8%)
  starting transfers between devices  11.9 us (5%)
  other arithmetic  4.11 us (2%)
  between operations  2.7 us (1%)
    unnamed x1, blocking collectives  159 us
    dot_general x1, matrix products, absorb(): jnp.dot(w_uv, w_out, precision=lax.Precision.HIGHEST, preferred_element_t...  15.4 us
    scatter x1, local copies, waits for them, and re-layouts, body(): outgoing = jnp.zeros((devcount * capacity, head_size, head_size), jnp.flo...  14.7 us
    all_to_all x1, starting transfers between devices, body(): lax.all_to_all(outgoing.reshape(devcount, capacity, head_size, head_size)...  11.9 us
    transpose x2, local copies, waits for them, and re-layouts, absorb(): blocks[qb + 2 * kb:].transpose(1, 0, 2).reshape(head_size, model_width)  9.57 us
    gather x1, local copies, waits for them, and re-layouts, body(): blocks = arrived[source * capacity + position]  6.52 us
  transfers between devices with their start and end apart: 1, of which 0 were waited for; matrix products, arithmetic and copies ran while one was open for 1% of the time, Pallas kernels for 0%

commit v1 on v0

v1 whole, which is shorter than its diff:
```python
import functools

import jax
import jax.numpy as jnp
from jax import lax
from jax.experimental import pallas as pl
from jax.experimental.pallas import tpu as pltpu
from jax.sharding import PartitionSpec as P

DH = 128
QL = 1536
KL = 512
D = 7168
HEADS = 128
BLOCKS = 76
SHARE = (QL + KL) // HEADS
MESH = pl.DeviceIdType.MESH

ROUTES = ((0, 1, 2), (1, 2, 0), (2, 0, 1))
STARTS = (0, 48, 88)
ROWS = (48, 40, 40)
HOPS = (1, 3, 2)


def position():
    dev = lax.axis_index("dev")
    return (lax.axis_index("grp"), dev // 8, (dev // 2) % 4, dev % 2)


def device(coords, core):
    x, z, y = coords
    return (x, z * 8 + y * 2 + core)


def shifted(coords, dim, by):
    moved = list(coords)
    moved[dim] = (moved[dim] + by) % 4
    return moved


def exchange_kernel(
    flat_hbm, gains_ref, place_ref, serve_ref,
    got0, got1, got2, gain_out, where_out,
    flat, tab_v, tab_s, own0, own1, own2, first0, first1, first2,
    second0, second1, second2, gather, load_sem, tab_sem, send_sem, recv_sem, home_sem,
):
    x, z, y, core = position()
    here = (x, z, y)
    me = x * 32 + z * 8 + y * 2 + core
    own, first, second, got = (
        (own0, own1, own2), (first0, first1, first2), (second0, second1, second2), (got0, got1, got2))

    load = pltpu.make_async_copy(flat_hbm, flat, load_sem)
    load.start()

    barrier = pltpu.get_barrier_semaphore()
    peers = [device(here, 1 - core)]
    for dim in range(3):
        for hop in HOPS:
            for c in (core, 1 - core):
                peers.append(device(shifted(here, dim, hop), c))
    for peer in peers:
        pl.semaphore_signal(barrier, inc=1, device_id=peer, device_id_type=MESH)

    place = place_ref[...]
    local = place - me * BLOCKS
    held = (local >= 0) & (local < BLOCKS)
    block_of_head = jnp.sum(jnp.where(held, local, 0), axis=1, keepdims=True)
    rank_of_head = jnp.transpose(jnp.broadcast_to(serve_ref[...], (HEADS, HEADS)))
    target = lax.broadcasted_iota(jnp.int32, (HEADS, HEADS), 1)
    tab_v[...] = jnp.sum(
        jnp.where(rank_of_head == target, block_of_head, 0), axis=0, keepdims=True)
    table = pltpu.make_async_copy(tab_v, tab_s, tab_sem)
    table.start()
    mine = jnp.sum(
        jnp.where(rank_of_head[:, :BLOCKS] == me, place, 0), axis=0, keepdims=True)
    source = (mine * 55189) >> 22
    away = ((x - (source >> 5)) & 3, (z - (source >> 3)) & 3, (y - (source >> 1)) & 3)
    for o, (d1, d2, d3) in enumerate(ROUTES):
        slot = ((away[d3] * 2 + (source & 1)) * 4 + away[d2]) * 4 + away[d1]
        where_out[pl.ds(o, 1), pl.ds(0, BLOCKS)] = slot

    gather[me] = gains_ref[...]

    table.wait()
    load.wait()

    def pack(i, carry):
        rx, rz, ry, c = i // 32, (i // 8) % 4, (i // 2) % 4, i % 2
        to = ((x + rx) % 4) * 32 + ((z + rz) % 4) * 8 + ((y + ry) % 4) * 2 + c
        block = tab_s[0, to]
        own0[rx, rz, ry, c] = flat[block, pl.ds(STARTS[0], ROWS[0])]
        own1[rz, ry, rx, c] = flat[block, pl.ds(STARTS[1], ROWS[1])]
        own2[ry, rx, rz, c] = flat[block, pl.ds(STARTS[2], ROWS[2])]
        return carry

    lax.fori_loop(0, HEADS, pack, 0)
    pl.semaphore_wait(barrier, len(peers))

    copies = []

    def send(src, dst, to):
        n = len(copies)
        copy = pltpu.make_async_remote_copy(
            src, dst, send_sem.at[n], recv_sem.at[n], device_id=to, device_id_type=MESH)
        copy.start()
        copies.append(copy)
        return copy

    into_first = {}
    for r in HOPS:
        for o, (d1, d2, d3) in enumerate(ROUTES):
            into_first[o, r] = send(
                own[o].at[r], first[o].at[r - 1], device(shifted(here, d1, r), core))
    gain_x = [send(gather.at[me], gather.at[me], device(shifted(here, 0, r), core)) for r in HOPS]
    into_second = {}
    for r in HOPS:
        for o, (d1, d2, d3) in enumerate(ROUTES):
            into_second[o, r, 0] = send(
                own[o].at[0, r], second[o].at[r - 1, 0], device(shifted(here, d2, r), core))

    for q in HOPS:
        for o, (d1, d2, d3) in enumerate(ROUTES):
            into_first[o, q].wait_recv()
            for r in HOPS:
                into_second[o, r, q] = send(
                    first[o].at[q - 1, r], second[o].at[r - 1, q],
                    device(shifted(here, d2, r), core))

    for copy in gain_x:
        copy.wait_recv()
    rows = [((x + k) % 4) * 32 + z * 8 + y * 2 + core for k in range(4)]
    gain_z = [
        send(gather.at[row], gather.at[row], device(shifted(here, 1, r), core))
        for r in HOPS for row in rows]

    final = []
    homes = []

    def deliver(o, src, dst_index):
        d3 = ROUTES[o][2]
        for r in (1, 3, 2, 0):
            for c in range(2):
                to_core = core if c == 0 else 1 - core
                a, b = src(r, to_core), got[o].at[(r, core) + dst_index]
                if r == 0 and c == 0:
                    copy = pltpu.make_async_copy(a, b, home_sem.at[len(homes)])
                    copy.start()
                    homes.append(copy)
                else:
                    final.append(send(a, b, device(shifted(here, d3, r), to_core)))

    for o in range(3):
        deliver(o, lambda r, c: own[o].at[0, 0, r, c], (0, 0))
        deliver(o, lambda r, c: first[o].at[:, 0, r, c], (0, pl.ds(1, 3)))

    for copy in gain_z:
        copy.wait_recv()
    gain_y = []
    for k in range(4):
        for l in range(4):
            row = ((x + k) % 4) * 32 + ((z + l) % 4) * 8 + y * 2 + core
            for r in (1, 3, 2, 0):
                for c in (core, 1 - core):
                    if r == 0 and c is core:
                        continue
                    gain_y.append(send(
                        gather.at[row], gather.at[row], device(shifted(here, 2, r), c)))

    for q in HOPS:
        for o in range(3):
            for r1 in range(4):
                into_second[o, q, r1].wait_recv()
            deliver(o, lambda r, c: second[o].at[q - 1, :, r, c], (q,))

    for copy in gain_y:
        copy.wait_recv()
    turned = jnp.transpose(gather[...].reshape(HEADS, HEADS))
    for d in range(HEADS):
        gain_out[pl.ds(d * SHARE, SHARE)] = jnp.broadcast_to(
            turned[:SHARE, d:d + 1], (SHARE, DH))

    for copy in final:
        copy.wait_recv()
    for copy in homes:
        copy.wait()
    for copy in copies:
        copy.wait_send()


def exchange(flat_master, gains, place, serve_rank):
    def parts(*lead):
        return [pltpu.VMEM(lead + (n, DH), jnp.float32) for n in ROWS]

    n_sends = 9 + 3 + 9 + 27 + 12 + 3 * 7 * 5 + 112
    return pl.pallas_call(
        exchange_kernel,
        out_shape=[jax.ShapeDtypeStruct((4, 2, 4, 4, n, DH), jnp.float32) for n in ROWS] + [
            jax.ShapeDtypeStruct((QL + KL, DH), jnp.float32),
            jax.ShapeDtypeStruct((8, 128), jnp.int32)],
        in_specs=[pl.BlockSpec(memory_space=pl.ANY)] + [pl.BlockSpec(memory_space=pltpu.VMEM)] * 3,
        out_specs=[pl.BlockSpec(memory_space=pl.ANY)] * 3 + [pl.BlockSpec(memory_space=pltpu.VMEM)] * 2,
        scratch_shapes=[
            pltpu.VMEM((BLOCKS, DH, DH), jnp.float32),
            pltpu.VMEM((1, HEADS), jnp.int32),
            pltpu.SMEM((1, HEADS), jnp.int32),
            *parts(4, 4, 4, 2), *parts(3, 4, 4, 2), *parts(3, 4, 4, 2),
            pltpu.VMEM((HEADS, 1, DH), jnp.float32),
            pltpu.SemaphoreType.DMA,
            pltpu.SemaphoreType.DMA,
            pltpu.SemaphoreType.DMA((n_sends,)),
            pltpu.SemaphoreType.DMA((n_sends,)),
            pltpu.SemaphoreType.DMA((15,)),
        ],
        compiler_params=pltpu.CompilerParams(
            collective_id=0, has_side_effects=True, vmem_limit_bytes=56 << 20),
        name="exchange",
    )(flat_master, gains, place, serve_rank)


def split(a):
    high = a.astype(jnp.bfloat16)
    return high, (a - high.astype(jnp.float32)).astype(jnp.bfloat16)


def product_kernel(where, got0, got1, got2, gain, qk_ref, vo_ref, uv, uk_high, uk_low):
    step = pl.program_id(0)

    def block(j):
        return jnp.concatenate(
            [got[where[o, j]] for o, got in enumerate((got0, got1, got2))], axis=0)

    @pl.when(step == 0)
    def _():
        for b in range(KL // DH):
            g = gain[pl.ds(QL + b * DH, DH)]
            high, low = split(block(QL // DH + b) * g)
            uk_high[pl.ds(b * DH, DH)] = jnp.concatenate([high, high], axis=1)
            uk_low[pl.ds(b * DH, DH)] = jnp.concatenate([low, low], axis=1)
            high, low = split(block((QL + KL) // DH + b) * g)
            uv[pl.ds(b * DH, DH)] = jnp.concatenate([high, low], axis=1)

    @pl.when(step < 6)
    def _():
        for b in range(2):
            j = step * 2 + b
            g = gain[pl.ds(pl.multiple_of(j * DH, DH), DH)]
            left = jnp.concatenate(split(block(j) * g), axis=1)
            dims = (((1,), (1,)), ((), ()))
            out = lax.dot_general(left, uk_high[...], dims, preferred_element_type=jnp.float32)
            out += lax.dot_general(left, uk_low[...], dims, preferred_element_type=jnp.float32)
            qk_ref[0, pl.ds(b * DH, DH)] = out.astype(jnp.bfloat16)

    for b in range(4):
        parts = [split(block((QL + 2 * KL) // DH + step * 8 + b * 2 + k)) for k in range(2)]
        high = jnp.concatenate([parts[0][0], parts[1][0]], axis=1)
        low = jnp.concatenate([parts[0][1], parts[1][1]], axis=1)
        out = jnp.dot(uv[...], jnp.concatenate([high, high], axis=0), preferred_element_type=jnp.float32)
        out += jnp.dot(uv[...], jnp.concatenate([low, low], axis=0), preferred_element_type=jnp.float32)
        vo_ref[0, :, pl.ds(b * 256, 256)] = out.astype(jnp.bfloat16)


def products(where, got, gain):
    return pl.pallas_call(
        product_kernel,
        grid_spec=pltpu.PrefetchScalarGridSpec(
            num_scalar_prefetch=1,
            grid=(7,),
            in_specs=[pl.BlockSpec(memory_space=pltpu.VMEM)] * 4,
            out_specs=[
                pl.BlockSpec((1, 256, KL), lambda i, w: (0, jnp.minimum(i, 5), 0)),
                pl.BlockSpec((1, KL, 1024), lambda i, w: (0, 0, i))],
            scratch_shapes=[pltpu.VMEM((KL, 2 * DH), jnp.bfloat16)] * 3,
        ),
        out_shape=[
            jax.ShapeDtypeStruct((1, QL, KL), jnp.bfloat16),
            jax.ShapeDtypeStruct((1, KL, D), jnp.bfloat16)],
        compiler_params=pltpu.CompilerParams(vmem_limit_bytes=56 << 20),
        name="products",
    )(where, *got, gain)


def body(flat_master, norm_gains, place, serve_rank):
    gains = jnp.pad(norm_gains[None], ((0, 0), (0, DH - SHARE)))
    *got, gain, where = exchange(flat_master, gains, place, serve_rank[None])
    got = [g.reshape(HEADS, n, DH) for g, n in zip(got, ROWS)]
    return tuple(products(where, got, gain))


def solution(mesh):
    in_specs = (P(("grp", "dev"), None, None), P(("grp", "dev")), P(), P())
    out_specs = (P(("grp", "dev"), None, None), P(("grp", "dev"), None, None))
    return jax.shard_map(body, mesh=mesh, in_specs=in_specs, out_specs=out_specs, check_vma=False)
```

time: 234 us -> 128 us (0.55)
  blocking collectives: 159 us -> 0 us
  Pallas kernels: 0 us -> 124 us
  local copies, waits for them, and re-layouts: 36.4 us -> 2.68 us
  matrix products: 19.2 us -> 0 us
  starting transfers between devices: 11.9 us -> 0 us
  other arithmetic: 4.11 us -> 0 us
    unnamed x1 -> x0, blocking collectives: 159 us -> none
    pallas_call x0 -> x2, Pallas kernels: none -> 124 us  [the longest x1 111 us: exchange(): pl.pallas_call(exchange_kernel, out_shape=[jax.ShapeDtypeStruct((4, 2, 4,...]
    dot_general x2 -> x0, matrix products: 19.2 us -> none  [the longest x1 15.4 us: absorb(): jnp.dot(w_uv, w_out, precision=lax.Precision.HIGHEST, preferred_element_t...]
    scatter x1 -> x0, local copies, waits for them, and re-layouts: 14.7 us -> none  [body(): outgoing = jnp.zeros((devcount * capacity, head_size, head_size), jnp.flo...]
    all_to_all x1 -> x0, starting transfers between devices: 11.9 us -> none  [body(): lax.all_to_all(outgoing.reshape(devcount, capacity, head_size, head_size)...]
    transpose x2 -> x0, local copies, waits for them, and re-layouts: 9.57 us -> none  [absorb(): blocks[qb + 2 * kb:].transpose(1, 0, 2).reshape(head_size, model_width)]
    gather x1 -> x0, local copies, waits for them, and re-layouts: 6.52 us -> none  [body(): blocks = arrived[source * capacity + position]]
    broadcast_in_dim x1 -> x0, local copies, waits for them, and re-layouts: 4.27 us -> none  [body(): jnp.zeros((devcount * capacity, head_size, head_size), jnp.float32)]
  transfers between devices with their start and end apart: 1 -> 0, of which waited for: 0 -> 0; matrix products, arithmetic and copies ran while one was open for 1% -> 0% of each run, Pallas kernels for 0% -> 0%
where the time goes in v1:
time: 128 us
  Pallas kernels  124 us (97%)
  local copies, waits for them, and re-layouts  2.68 us (2%)
    pallas_call x1, Pallas kernels, exchange(): pl.pallas_call(exchange_kernel, out_shape=[jax.ShapeDtypeStruct((4, 2, 4,...  111 us
    pallas_call x1, Pallas kernels, products(): pl.pallas_call(product_kernel, grid_spec=pltpu.PrefetchScalarGridSpec(num...  13.8 us

profile of v1, /device:TPU:1, one launch (start us, length us, event | category | flops | bytes accessed | tf_op | source)
XLA Modules:
  0.0 127.7 jit_solution(11265991085280861108)
XLA Ops:
  0.6 1.2 pad.4.gains_ref
  1.8 1.5 %copy.6.place_ref = s32[128,76]{1,0:T(8,128)} copy(s32[128,76]{0,1:T(8,128)} %param.6) | data formatting | bytes 77824 | tf_op args[2]
  3.3 110.7 %exchange.1 = (f32[4,2,4,4,48,128]{5,4,3,2,1,0:T(8,128)}, f32[4,2,4,4,40,128]{5,4,3,2,1,0:T(8,128)}, f32[4,2,4,4,40,128]{5,4,3,2,1,0:T(8,128)}, f32[2048,128]{1,0:T(8,128)}, s32[8,128]{1,0:T(8,128)}) custom-call(f32[76,128,128]{2,1,0:T(8,128)} %flat_hbm.1, f32[1,128]{1,0:T(1,128)} %pad.4.gains_ref, s32[128,76]{1,0:T(8,128)} %copy.6.place_ref, s32[1,128]{1,0:T(1,128)} %bitcast.8), custom_call_target="tpu_custom_call" | custom-call | tf_op jit(solution)/shard_map/exchange/pallas_call | solution.py:196
  114.0 13.8 %products.1 = (bf16[1,1536,512]{2,1,0:T(8,128)(2,1)}, bf16[1,512,7168]{2,1,0:T(8,128)(2,1)}) custom-call(s32[8,128]{1,0:T(8,128)} %get-tuple-element.7.where, f32[128,48,128]{2,1,0:T(8,128)} %bitcast.5, f32[128,40,128]{2,1,0:T(8,128)} %bitcast.6, f32[128,40,128]{2,1,0:T(8,128)} %bitcast.7, f32[2048,128]{1,0:T(8,128)} %get-tuple-element.11.gain), custom_call_target="tpu_custom_call" | custom-call | tf_op jit(solution)/shard_map/products/pallas_call | solution.py:264

commit v2 on v1

v2 whole, which is shorter than its diff:
```python
import jax
import jax.numpy as jnp
from jax import lax
from jax.experimental import pallas as pl
from jax.experimental.pallas import tpu as pltpu
from jax.sharding import PartitionSpec as P

DH = 128
QL = 1536
KL = 512
D = 7168
HEADS = 128
BLOCKS = 76
SHARE = (QL + KL) // HEADS
STRIP = 512
MESH = pl.DeviceIdType.MESH

ROUTES = ((0, 1, 2), (1, 2, 0), (2, 0, 1))
STARTS = (0, 48, 88)
ROWS = (48, 40, 40)
HOPS = (1, 3, 2)


def position():
    dev = lax.axis_index("dev")
    return (lax.axis_index("grp"), dev // 8, (dev // 2) % 4, dev % 2)


def device(coords, core):
    x, z, y = coords
    return (x, z * 8 + y * 2 + core)


def shifted(coords, dim, by):
    moved = list(coords)
    moved[dim] = (moved[dim] + by) % 4
    return moved


def exchange_kernel(
    flat_hbm, gains_hbm, place_hbm, serve_hbm,
    got0, got1, got2, gain_out, where_out,
    flat, gains_ref, place_ref, serve_ref, tab_v, tab_s,
    own0, own1, own2, first0, first1, first2, second0, second1, second2, gather,
    load_sem, tab_sem, first_sem, second_sem, got_sem, gain_sem,
    sent_first, sent_second, sent_got, sent_core, sent_gain,
):
    x, z, y, core = position()
    here = (x, z, y)
    me = x * 32 + z * 8 + y * 2 + core
    own, first, second, got = (
        (own0, own1, own2), (first0, first1, first2), (second0, second1, second2), (got0, got1, got2))

    loads = [
        pltpu.make_async_copy(src, dst, load_sem.at[n]) for n, (src, dst) in enumerate((
            (place_hbm, place_ref), (serve_hbm, serve_ref), (gains_hbm, gains_ref),
            (flat_hbm, flat)))]
    for load in loads:
        load.start()

    barrier = pltpu.get_barrier_semaphore()
    peers = [device(here, 1 - core)]
    for dim in range(3):
        for hop in HOPS:
            for c in (core, 1 - core):
                peers.append(device(shifted(here, dim, hop), c))
    for peer in peers:
        pl.semaphore_signal(barrier, inc=1, device_id=peer, device_id_type=MESH)

    for load in loads[:3]:
        load.wait()
    place = place_ref[...]
    local = place - me * BLOCKS
    held = (local >= 0) & (local < BLOCKS)
    block_of_head = jnp.sum(jnp.where(held, local, 0), axis=0, keepdims=True)
    pairs = jnp.broadcast_to(serve_ref[...] * 128 + block_of_head, (HEADS, HEADS))
    pairs = jnp.transpose(pairs)
    target = lax.broadcasted_iota(jnp.int32, (HEADS, HEADS), 1)
    tab_v[...] = jnp.sum(
        jnp.where(pairs >> 7 == target, pairs & 127, 0), axis=0, keepdims=True)
    table = pltpu.make_async_copy(tab_v, tab_s, tab_sem)
    table.start()
    gather[x, z, y, core] = jnp.concatenate(
        [gains_ref[...], jnp.zeros((1, DH - SHARE), jnp.float32)], axis=1)
    table.wait()
    loads[3].wait()
    pl.semaphore_wait(barrier, len(peers))

    def pack(o, r):
        d1, d2, d3 = ROUTES[o]
        dst = own[o].at[r - 1] if r else first[o].at[0]

        def one(i, carry):
            a, b, c = i // 8, (i // 2) % 4, i % 2
            to = [None] * 3
            to[d1], to[d2], to[d3] = (here[d1] + r) % 4, (here[d2] + a) % 4, (here[d3] + b) % 4
            block = tab_s[0, to[0] * 32 + to[1] * 8 + to[2] * 2 + c]
            dst[a, b, c] = flat[block, pl.ds(STARTS[o], ROWS[o])]
            return carry

        lax.fori_loop(0, 32, one, 0, unroll=8)

    def send(src, dst, sent, landed, to):
        pltpu.make_async_remote_copy(
            src, dst, sent, landed, device_id=to, device_id_type=MESH).start()

    def await_bytes(ref, sem):
        pltpu.make_async_copy(ref, ref, sem).wait()

    for r in HOPS:
        for o, (d1, d2, d3) in enumerate(ROUTES):
            pack(o, r)
            send(own[o].at[r - 1], first[o].at[r], sent_first.at[o], first_sem.at[o, r - 1],
                 device(shifted(here, d1, r), core))
    mine = gather.at[x, z, y, core]
    for r in HOPS:
        send(mine, mine, sent_gain.at[0], gain_sem.at[0], device(shifted(here, 0, r), core))

    def forward(o, q):
        d2 = ROUTES[o][1]
        for r in HOPS:
            send(first[o].at[q, r], second[o].at[r - 1, q], sent_second.at[o],
                 second_sem.at[o, r - 1], device(shifted(here, d2, r), core))

    for o in range(3):
        pack(o, 0)
        forward(o, 0)

    wanted = jnp.sum(jnp.where(serve_ref[...] == me, place_ref[...], 0), axis=1, keepdims=True)
    wanted = jnp.transpose(jnp.broadcast_to(wanted, (BLOCKS, HEADS)))[:1]
    source = (wanted * 55189) >> 22
    away = ((x - (source >> 5)) & 3, (z - (source >> 3)) & 3, (y - (source >> 1)) & 3)
    for o, (d1, d2, d3) in enumerate(ROUTES):
        slot = ((away[d3] * 2 + (source & 1)) * 4 + away[d2]) * 4 + away[d1]
        where_out[pl.ds(o, 1), pl.ds(0, BLOCKS)] = slot

    for q in HOPS:
        for o in range(3):
            await_bytes(first[o].at[q], first_sem.at[o, q - 1])
            forward(o, q)

    await_bytes(gather.at[0, 0, pl.ds(0, 3), 0], gain_sem.at[0])
    mine = gather.at[:, z, y, core]
    for r in HOPS:
        send(mine, mine, sent_gain.at[1], gain_sem.at[1], device(shifted(here, 1, r), core))

    def deliver(o, src, q):
        d3 = ROUTES[o][2]
        for r in (1, 3, 2, 0):
            for c in (0, 1):
                to_core = (core + c) % 2
                a, b = src.at[:, r, to_core], got[o].at[r, core, q]
                if r == 0 and c == 0:
                    pltpu.make_async_copy(a, b, got_sem.at[o]).start()
                else:
                    send(a, b, sent_got.at[o] if r else sent_core.at[o], got_sem.at[o],
                         device(shifted(here, d3, r), to_core))

    for o in range(3):
        deliver(o, first[o].at[:, 0], 0)

    await_bytes(gather.at[pl.ds(0, 3), 0, :, 0], gain_sem.at[1])
    mine = gather.at[:, :, y, core]
    for r in (1, 3, 2, 0):
        for c in (0, 1):
            if r or c:
                n = 2 if r else 3
                send(mine, mine, sent_gain.at[n], gain_sem.at[n],
                     device(shifted(here, 2, r), (core + c) % 2))

    for q in HOPS:
        for o in range(3):
            await_bytes(second[o].at[q - 1], second_sem.at[o, q - 1])
            deliver(o, second[o].at[q - 1], q)

    rest = gather.at[:, :, pl.ds(0, 3)]
    await_bytes(rest, gain_sem.at[2])
    await_bytes(gather.at[:, :, 3, 0], gain_sem.at[3])
    turned = jnp.transpose(gather[...].reshape(HEADS, HEADS))
    for d in range(HEADS):
        gain_out[pl.ds(d * SHARE, SHARE)] = jnp.broadcast_to(
            turned[:SHARE, d:d + 1], (SHARE, DH))

    for o in range(3):
        await_bytes(got[o], got_sem.at[o])
    for o in range(3):
        await_bytes(first[o].at[pl.ds(1, 3)], sent_first.at[o])
        await_bytes(second[o], sent_second.at[o])
        await_bytes(got[o].at[pl.ds(1, 3)], sent_got.at[o])
        await_bytes(got[o].at[0, 0], sent_core.at[o])
    await_bytes(gather.at[0, 0, pl.ds(0, 3), 0], sent_gain.at[0])
    await_bytes(gather.at[pl.ds(0, 3), 0, :, 0], sent_gain.at[1])
    await_bytes(rest, sent_gain.at[2])
    await_bytes(gather.at[:, :, 3, 0], sent_gain.at[3])


def exchange(flat_master, gains, place, serve_rank):
    def parts(*lead):
        return [pltpu.VMEM(lead + (n, DH), jnp.float32) for n in ROWS]

    dma = pltpu.SemaphoreType.DMA
    return pl.pallas_call(
        exchange_kernel,
        out_shape=parts(4, 2, 4, 4) + [
            pltpu.VMEM((QL + KL, DH), jnp.float32),
            pltpu.VMEM((8, 128), jnp.int32)],
        in_specs=[pl.BlockSpec(memory_space=pltpu.HBM)] * 4,
        out_specs=[pl.BlockSpec(memory_space=pltpu.VMEM)] * 5,
        scratch_shapes=[
            pltpu.VMEM((BLOCKS, DH, DH), jnp.float32),
            pltpu.VMEM((1, SHARE), jnp.float32),
            pltpu.VMEM((BLOCKS, HEADS), jnp.int32),
            pltpu.VMEM((1, HEADS), jnp.int32),
            pltpu.VMEM((1, HEADS), jnp.int32),
            pltpu.SMEM((1, HEADS), jnp.int32),
            *parts(3, 4, 4, 2), *parts(4, 4, 4, 2), *parts(3, 4, 4, 2),
            pltpu.VMEM((4, 4, 4, 2, 1, DH), jnp.float32),
            dma((4,)), dma, dma((3, 3)), dma((3, 3)), dma((3,)), dma((4,)),
            dma((3,)), dma((3,)), dma((3,)), dma((3,)), dma((4,)),
        ],
        compiler_params=pltpu.CompilerParams(
            collective_id=0, has_side_effects=True, vmem_limit_bytes=52 << 20),
        name="exchange",
    )(flat_master, gains, place, serve_rank)


def split(a):
    high = a.astype(jnp.bfloat16)
    return high, (a - high.astype(jnp.float32)).astype(jnp.bfloat16)


def product_kernel(where, got0, got1, got2, gain, qk_hbm, vo_hbm, uv, uk, qk, vo, sems):
    def block(j):
        return jnp.concatenate(
            [got[where[o, j]] for o, got in enumerate((got0, got1, got2))], axis=0)

    copies = []

    def write(src, dst):
        copy = pltpu.make_async_copy(src, dst, sems.at[len(copies)])
        copy.start()
        copies.append(copy)

    for b in range(KL // DH):
        rows = pl.ds(b * DH, DH)
        g = gain[pl.ds(QL + b * DH, DH)]
        high, low = split(block((QL + KL) // DH + b) * g)
        uv[rows] = jnp.concatenate([high, low, high], axis=1)
        high, low = split(jnp.transpose(block(QL // DH + b) * g))
        uk[:, rows] = jnp.concatenate([high, high, low], axis=0)

    for start in range(0, D, STRIP):
        for column in range(start, start + STRIP, 2 * DH):
            j = (QL + 2 * KL + column) // DH
            (high0, low0), (high1, low1) = split(block(j)), split(block(j + 1))
            high = jnp.concatenate([high0, high1], axis=1)
            low = jnp.concatenate([low0, low1], axis=1)
            out = jnp.dot(
                uv[...], jnp.concatenate([high, high, low], axis=0),
                preferred_element_type=jnp.float32)
            vo[:, pl.ds(column, 2 * DH)] = out.astype(jnp.bfloat16)
        strip = pl.ds(start, STRIP)
        write(vo.at[:, strip], vo_hbm.at[0, :, strip])

    for start in range(0, QL, KL):
        left = []
        for row in range(start, start + KL, DH):
            high, low = split(block(row // DH) * gain[pl.ds(row, DH)])
            left.append(jnp.concatenate([high, low, high], axis=1))
        left = jnp.concatenate(left, axis=0)
        rows = pl.ds(start, KL)
        for column in range(0, KL, 2 * DH):
            out = jnp.dot(
                left, uk[:, pl.ds(column, 2 * DH)], preferred_element_type=jnp.float32)
            qk[rows, pl.ds(column, 2 * DH)] = out.astype(jnp.bfloat16)
        write(qk.at[rows], qk_hbm.at[0, rows])

    for copy in copies:
        copy.wait()


def products(where, got, gain):
    return pl.pallas_call(
        product_kernel,
        in_specs=[pl.BlockSpec(memory_space=pltpu.SMEM)]
        + [pl.BlockSpec(memory_space=pltpu.VMEM)] * 4,
        out_specs=[pl.BlockSpec(memory_space=pl.ANY)] * 2,
        scratch_shapes=[
            pltpu.VMEM((KL, 3 * DH), jnp.bfloat16),
            pltpu.VMEM((3 * DH, KL), jnp.bfloat16),
            pltpu.VMEM((QL, KL), jnp.bfloat16),
            pltpu.VMEM((KL, D), jnp.bfloat16),
            pltpu.SemaphoreType.DMA((D // STRIP + QL // KL,)),
        ],
        out_shape=[
            jax.ShapeDtypeStruct((1, QL, KL), jnp.bfloat16),
            jax.ShapeDtypeStruct((1, KL, D), jnp.bfloat16)],
        compiler_params=pltpu.CompilerParams(vmem_limit_bytes=32 << 20),
        name="products",
    )(where, *got, gain)


def body(flat_master, norm_gains, place, serve_rank):
    *got, gain, where = exchange(flat_master, norm_gains[None], place.T, serve_rank[None])
    got = [g.reshape(HEADS, n, DH) for g, n in zip(got, ROWS)]
    return tuple(products(where, got, gain))


def solution(mesh):
    in_specs = (P(("grp", "dev"), None, None), P(("grp", "dev")), P(), P())
    out_specs = (P(("grp", "dev"), None, None), P(("grp", "dev"), None, None))
    return jax.shard_map(body, mesh=mesh, in_specs=in_specs, out_specs=out_specs, check_vma=False)
```

time: 128 us -> 110 us (0.86)
  Pallas kernels: 124 us -> 109 us
  local copies, waits for them, and re-layouts: 2.68 us -> 0 us
    pallas_call x2, Pallas kernels: 124 us -> 109 us  [the longest x1 102 us: exchange(): pl.pallas_call(exchange_kernel, out_shape=parts(4, 2, 4, 4) + [pltpu.VMEM...]
    unnamed x1 -> x0, local copies, waits for them, and re-layouts: 1.51 us -> none
where the time goes in v2:
time: 110 us; the launch traced here: 109 us
  Pallas kernels  109 us (99%)
    pallas_call x1, Pallas kernels, exchange(): pl.pallas_call(exchange_kernel, out_shape=parts(4, 2, 4, 4) + [pltpu.VMEM...  102 us
    pallas_call x1, Pallas kernels, products(): pl.pallas_call(product_kernel, in_specs=[pl.BlockSpec(memory_space=pltpu....  6.43 us

profile of v2, /device:TPU:1, one launch (start us, length us, event | category | flops | bytes accessed | tf_op | source)
XLA Modules:
  0.0 109.4 jit_solution(5290164985147925272)
XLA Ops:
  0.6 102.4 %exchange.1 = (f32[4,2,4,4,48,128]{5,4,3,2,1,0:T(8,128)S(1)}, f32[4,2,4,4,40,128]{5,4,3,2,1,0:T(8,128)S(1)}, f32[4,2,4,4,40,128]{5,4,3,2,1,0:T(8,128)S(1)}, f32[2048,128]{1,0:T(8,128)S(1)}, s32[8,128]{1,0:T(8,128)S(1)}) custom-call(f32[76,128,128]{2,1,0:T(8,128)} %flat_hbm.1, f32[1,16]{1,0:T(1,128)} %bitcast.10, s32[76,128]{1,0:T(8,128)} %bitcast.9, ...), custom_call_target="tpu_custom_call" | custom-call | tf_op jit(solution)/shard_map/exchange/pallas_call | solution.py:202
  103.0 6.4 %products.1 = (bf16[1,1536,512]{2,1,0:T(8,128)(2,1)}, bf16[1,512,7168]{2,1,0:T(8,128)(2,1)}) custom-call(s32[8,128]{1,0:T(8,128)S(1)} %get-tuple-element.7.where, f32[128,48,128]{2,1,0:T(8,128)S(1)} %bitcast.6, f32[128,40,128]{2,1,0:T(8,128)S(1)} %bitcast.7, f32[128,40,128]{2,1,0:T(8,128)S(1)} %bitcast.8, f32[2048,128]{1,0:T(8,128)S(1)} %get-tuple-element.11.gain), custom_call_target="tpu_custom_call" | custom-call | tf_op jit(solution)/shard_map/products/pallas_call | solution.py:283

commit v3 on v2

--- a/solution.py
+++ b/solution.py
@@ -13,6 +13,7 @@
 BLOCKS = 76
 SHARE = (QL + KL) // HEADS
 STRIP = 512
+PIECE = 19
 MESH = pl.DeviceIdType.MESH
 
 ROUTES = ((0, 1, 2), (1, 2, 0), (2, 0, 1))
@@ -40,9 +41,9 @@
 def exchange_kernel(
     flat_hbm, gains_hbm, place_hbm, serve_hbm,
     got0, got1, got2, gain_out, where_out,
-    flat, gains_ref, place_ref, serve_ref, tab_v, tab_s,
+    gain, where, flat, gains_ref, place_ref, serve_ref, tab_v, tab_s,
     own0, own1, own2, first0, first1, first2, second0, second1, second2, gather,
-    load_sem, tab_sem, first_sem, second_sem, got_sem, gain_sem,
+    load_sem, tab_sem, out_sem, first_sem, second_sem, got_sem, gain_sem,
     sent_first, sent_second, sent_got, sent_core, sent_gain,
 ):
     x, z, y, core = position()
@@ -53,8 +54,9 @@
 
     loads = [
         pltpu.make_async_copy(src, dst, load_sem.at[n]) for n, (src, dst) in enumerate((
-            (place_hbm, place_ref), (serve_hbm, serve_ref), (gains_hbm, gains_ref),
-            (flat_hbm, flat)))]
+            (place_hbm, place_ref), (serve_hbm, serve_ref), (gains_hbm, gains_ref)) + tuple(
+            (flat_hbm.at[pl.ds(start, PIECE)], flat.at[pl.ds(start, PIECE)])
+            for start in range(0, BLOCKS, PIECE)))]
     for load in loads:
         load.start()
 
@@ -83,8 +85,8 @@
     gather[x, z, y, core] = jnp.concatenate(
         [gains_ref[...], jnp.zeros((1, DH - SHARE), jnp.float32)], axis=1)
     table.wait()
-    loads[3].wait()
-    pl.semaphore_wait(barrier, len(peers))
+    for load in loads[3:]:
+        load.wait()
 
     def pack(o, r):
         d1, d2, d3 = ROUTES[o]
@@ -107,9 +109,13 @@
     def await_bytes(ref, sem):
         pltpu.make_async_copy(ref, ref, sem).wait()
 
+    for o in range(3):
+        pack(o, HOPS[0])
+    pl.semaphore_wait(barrier, len(peers))
     for r in HOPS:
         for o, (d1, d2, d3) in enumerate(ROUTES):
-            pack(o, r)
+            if r != HOPS[0]:
+                pack(o, r)
             send(own[o].at[r - 1], first[o].at[r], sent_first.at[o], first_sem.at[o, r - 1],
                  device(shifted(here, d1, r), core))
     mine = gather.at[x, z, y, core]
@@ -132,7 +138,9 @@
     away = ((x - (source >> 5)) & 3, (z - (source >> 3)) & 3, (y - (source >> 1)) & 3)
     for o, (d1, d2, d3) in enumerate(ROUTES):
         slot = ((away[d3] * 2 + (source & 1)) * 4 + away[d2]) * 4 + away[d1]
-        where_out[pl.ds(o, 1), pl.ds(0, BLOCKS)] = slot
+        where[pl.ds(o, 1), pl.ds(0, BLOCKS)] = slot
+    where_copy = pltpu.make_async_copy(where, where_out, out_sem.at[0])
+    where_copy.start()
 
     for q in HOPS:
         for o in range(3):
@@ -168,19 +176,26 @@
                 send(mine, mine, sent_gain.at[n], gain_sem.at[n],
                      device(shifted(here, 2, r), (core + c) % 2))
 
-    for q in HOPS:
+    def finish(q):
         for o in range(3):
             await_bytes(second[o].at[q - 1], second_sem.at[o, q - 1])
             deliver(o, second[o].at[q - 1], q)
 
+    finish(HOPS[0])
+    finish(HOPS[1])
     rest = gather.at[:, :, pl.ds(0, 3)]
     await_bytes(rest, gain_sem.at[2])
     await_bytes(gather.at[:, :, 3, 0], gain_sem.at[3])
     turned = jnp.transpose(gather[...].reshape(HEADS, HEADS))
     for d in range(HEADS):
-        gain_out[pl.ds(d * SHARE, SHARE)] = jnp.broadcast_to(
+        gain[pl.ds(d * SHARE, SHARE)] = jnp.broadcast_to(
             turned[:SHARE, d:d + 1], (SHARE, DH))
-
+    gain_copy = pltpu.make_async_copy(gain, gain_out, out_sem.at[1])
+    gain_copy.start()
+    finish(HOPS[2])
+
+    where_copy.wait()
+    gain_copy.wait()
     for o in range(3):
         await_bytes(got[o], got_sem.at[o])
     for o in range(3):
@@ -205,8 +220,10 @@
             pltpu.VMEM((QL + KL, DH), jnp.float32),
             pltpu.VMEM((8, 128), jnp.int32)],
         in_specs=[pl.BlockSpec(memory_space=pltpu.HBM)] * 4,
-        out_specs=[pl.BlockSpec(memory_space=pltpu.VMEM)] * 5,
+        out_specs=[pl.BlockSpec(memory_space=pl.ANY)] * 5,
         scratch_shapes=[
+            pltpu.VMEM((QL + KL, DH), jnp.float32),
+            pltpu.VMEM((8, 128), jnp.int32),
             pltpu.VMEM((BLOCKS, DH, DH), jnp.float32),
             pltpu.VMEM((1, SHARE), jnp.float32),
             pltpu.VMEM((BLOCKS, HEADS), jnp.int32),
@@ -215,7 +232,7 @@
             pltpu.SMEM((1, HEADS), jnp.int32),
             *parts(3, 4, 4, 2), *parts(4, 4, 4, 2), *parts(3, 4, 4, 2),
             pltpu.VMEM((4, 4, 4, 2, 1, DH), jnp.float32),
-            dma((4,)), dma, dma((3, 3)), dma((3, 3)), dma((3,)), dma((4,)),
+            dma((3 + BLOCKS // PIECE,)), dma, dma((2,)), dma((3, 3)), dma((3, 3)), dma((3,)), dma((4,)),
             dma((3,)), dma((3,)), dma((3,)), dma((3,)), dma((4,)),
         ],
         compiler_params=pltpu.CompilerParams(

time: 110 us -> 109 us (level)
    pallas_call x1, Pallas kernels: 102 us -> 101 us  [exchange(): pl.pallas_call(exchange_kernel, out_shape=parts(4, 2, 4, 4) + [pltpu.VMEM...]
where the time goes in v3:
time: 109 us; the launch traced here: 108 us
  Pallas kernels  108 us (99%)
    pallas_call x1, Pallas kernels, exchange(): pl.pallas_call(exchange_kernel, out_shape=parts(4, 2, 4, 4) + [pltpu.VMEM...  101 us
    pallas_call x1, Pallas kernels, products(): pl.pallas_call(product_kernel, in_specs=[pl.BlockSpec(memory_space=pltpu....  6.43 us

profile of v3, /device:TPU:1, one launch (start us, length us, event | category | flops | bytes accessed | tf_op | source)
XLA Modules:
  0.0 108.2 jit_solution(16793276855656263339)
XLA Ops:
  0.6 101.2 %exchange.1 = (f32[4,2,4,4,48,128]{5,4,3,2,1,0:T(8,128)S(1)}, f32[4,2,4,4,40,128]{5,4,3,2,1,0:T(8,128)S(1)}, f32[4,2,4,4,40,128]{5,4,3,2,1,0:T(8,128)S(1)}, f32[2048,128]{1,0:T(8,128)S(1)}, s32[8,128]{1,0:T(8,128)S(1)}) custom-call(f32[76,128,128]{2,1,0:T(8,128)} %flat_hbm.1, f32[1,16]{1,0:T(1,128)} %bitcast.10, s32[76,128]{1,0:T(8,128)} %bitcast.9, ...), custom_call_target="tpu_custom_call" | custom-call | tf_op jit(solution)/shard_map/exchange/pallas_call | solution.py:217
  101.8 6.4 %products.1 = (bf16[1,1536,512]{2,1,0:T(8,128)(2,1)}, bf16[1,512,7168]{2,1,0:T(8,128)(2,1)}) custom-call(s32[8,128]{1,0:T(8,128)S(1)} %get-tuple-element.7.where, f32[128,48,128]{2,1,0:T(8,128)S(1)} %bitcast.6, f32[128,40,128]{2,1,0:T(8,128)S(1)} %bitcast.7, f32[128,40,128]{2,1,0:T(8,128)S(1)} %bitcast.8, f32[2048,128]{1,0:T(8,128)S(1)} %get-tuple-element.11.gain), custom_call_target="tpu_custom_call" | custom-call | tf_op jit(solution)/shard_map/products/pallas_call | solution.py:300

commit v4 on v3

--- a/solution.py
+++ b/solution.py
@@ -13,13 +13,12 @@
 BLOCKS = 76
 SHARE = (QL + KL) // HEADS
 STRIP = 512
-PIECE = 19
 MESH = pl.DeviceIdType.MESH
 
 ROUTES = ((0, 1, 2), (1, 2, 0), (2, 0, 1))
 STARTS = (0, 48, 88)
 ROWS = (48, 40, 40)
-HOPS = (1, 3, 2)
+HOPS = (2, 1, 3)
 
 
 def position():
@@ -41,7 +40,7 @@
 def exchange_kernel(
     flat_hbm, gains_hbm, place_hbm, serve_hbm,
     got0, got1, got2, gain_out, where_out,
-    gain, where, flat, gains_ref, place_ref, serve_ref, tab_v, tab_s,
+    gain, where, flat0, flat1, flat2, gains_ref, place_ref, serve_ref, tab_v, tab_s,
     own0, own1, own2, first0, first1, first2, second0, second1, second2, gather,
     load_sem, tab_sem, out_sem, first_sem, second_sem, got_sem, gain_sem,
     sent_first, sent_second, sent_got, sent_core, sent_gain,
@@ -49,14 +48,15 @@
     x, z, y, core = position()
     here = (x, z, y)
     me = x * 32 + z * 8 + y * 2 + core
-    own, first, second, got = (
-        (own0, own1, own2), (first0, first1, first2), (second0, second1, second2), (got0, got1, got2))
+    flat, own, first, second, got = (
+        (flat0, flat1, flat2), (own0, own1, own2), (first0, first1, first2), (second0, second1, second2),
+        (got0, got1, got2))
 
     loads = [
         pltpu.make_async_copy(src, dst, load_sem.at[n]) for n, (src, dst) in enumerate((
             (place_hbm, place_ref), (serve_hbm, serve_ref), (gains_hbm, gains_ref)) + tuple(
-            (flat_hbm.at[pl.ds(start, PIECE)], flat.at[pl.ds(start, PIECE)])
-            for start in range(0, BLOCKS, PIECE)))]
+            (flat_hbm.at[:, pl.ds(start, n)], part)
+            for start, n, part in zip(STARTS, ROWS, flat)))]
     for load in loads:
         load.start()
 
@@ -85,22 +85,17 @@
     gather[x, z, y, core] = jnp.concatenate(
         [gains_ref[...], jnp.zeros((1, DH - SHARE), jnp.float32)], axis=1)
     table.wait()
-    for load in loads[3:]:
-        load.wait()
-
-    def pack(o, r):
+
+    def pack(o, r, q):
         d1, d2, d3 = ROUTES[o]
-        dst = own[o].at[r - 1] if r else first[o].at[0]
-
-        def one(i, carry):
-            a, b, c = i // 8, (i // 2) % 4, i % 2
-            to = [None] * 3
-            to[d1], to[d2], to[d3] = (here[d1] + r) % 4, (here[d2] + a) % 4, (here[d3] + b) % 4
-            block = tab_s[0, to[0] * 32 + to[1] * 8 + to[2] * 2 + c]
-            dst[a, b, c] = flat[block, pl.ds(STARTS[o], ROWS[o])]
-            return carry
-
-        lax.fori_loop(0, 32, one, 0, unroll=8)
+        dst = own[o].at[r - 1, q] if r else first[o].at[0, q]
+        to = [None] * 3
+        to[d1], to[d2] = (here[d1] + r) % 4, (here[d2] + q) % 4
+        for b in range(4):
+            to[d3] = (here[d3] + b) % 4
+            for c in range(2):
+                block = tab_s[0, to[0] * 32 + to[1] * 8 + to[2] * 2 + c]
+                dst[b, c] = flat[o][block]
 
     def send(src, dst, sent, landed, to):
         pltpu.make_async_remote_copy(
@@ -109,15 +104,16 @@
     def await_bytes(ref, sem):
         pltpu.make_async_copy(ref, ref, sem).wait()
 
-    for o in range(3):
-        pack(o, HOPS[0])
-    pl.semaphore_wait(barrier, len(peers))
     for r in HOPS:
-        for o, (d1, d2, d3) in enumerate(ROUTES):
-            if r != HOPS[0]:
-                pack(o, r)
+        for o in range(3):
+            if r == HOPS[0]:
+                loads[3 + o].wait()
+            for q in range(4):
+                pack(o, r, q)
+            if (o, r) == (0, HOPS[0]):
+                pl.semaphore_wait(barrier, len(peers))
             send(own[o].at[r - 1], first[o].at[r], sent_first.at[o], first_sem.at[o, r - 1],
-                 device(shifted(here, d1, r), core))
+                 device(shifted(here, ROUTES[o][0], r), core))
     mine = gather.at[x, z, y, core]
     for r in HOPS:
         send(mine, mine, sent_gain.at[0], gain_sem.at[0], device(shifted(here, 0, r), core))
@@ -129,7 +125,8 @@
                  second_sem.at[o, r - 1], device(shifted(here, d2, r), core))
 
     for o in range(3):
-        pack(o, 0)
+        for q in range(4):
+            pack(o, 0, q)
         forward(o, 0)
 
     wanted = jnp.sum(jnp.where(serve_ref[...] == me, place_ref[...], 0), axis=1, keepdims=True)
@@ -154,7 +151,7 @@
 
     def deliver(o, src, q):
         d3 = ROUTES[o][2]
-        for r in (1, 3, 2, 0):
+        for r in HOPS + (0,):
             for c in (0, 1):
                 to_core = (core + c) % 2
                 a, b = src.at[:, r, to_core], got[o].at[r, core, q]
@@ -224,7 +221,7 @@
         scratch_shapes=[
             pltpu.VMEM((QL + KL, DH), jnp.float32),
             pltpu.VMEM((8, 128), jnp.int32),
-            pltpu.VMEM((BLOCKS, DH, DH), jnp.float32),
+            *parts(BLOCKS),
             pltpu.VMEM((1, SHARE), jnp.float32),
             pltpu.VMEM((BLOCKS, HEADS), jnp.int32),
             pltpu.VMEM((1, HEADS), jnp.int32),
@@ -232,7 +229,7 @@
             pltpu.SMEM((1, HEADS), jnp.int32),
             *parts(3, 4, 4, 2), *parts(4, 4, 4, 2), *parts(3, 4, 4, 2),
             pltpu.VMEM((4, 4, 4, 2, 1, DH), jnp.float32),
-            dma((3 + BLOCKS // PIECE,)), dma, dma((2,)), dma((3, 3)), dma((3, 3)), dma((3,)), dma((4,)),
+            dma((6,)), dma, dma((2,)), dma((3, 3)), dma((3, 3)), dma((3,)), dma((4,)),
             dma((3,)), dma((3,)), dma((3,)), dma((3,)), dma((4,)),
         ],
         compiler_params=pltpu.CompilerParams(

time: 109 us -> 109 us (level)
  no operation moved by 1% of the time
where the time goes in v4:
time: 109 us; the launch traced here: 108 us
  Pallas kernels  108 us (99%)
    pallas_call x1, Pallas kernels, exchange(): pl.pallas_call(exchange_kernel, out_shape=parts(4, 2, 4, 4) + [pltpu.VMEM...  101 us
    pallas_call x1, Pallas kernels, products(): pl.pallas_call(product_kernel, in_specs=[pl.BlockSpec(memory_space=pltpu....  6.44 us

profile of v4, /device:TPU:1, one launch (start us, length us, event | category | flops | bytes accessed | tf_op | source)
XLA Modules:
  0.0 108.4 jit_solution(13755691548588631737)
XLA Ops:
  0.6 101.3 %exchange.1 = (f32[4,2,4,4,48,128]{5,4,3,2,1,0:T(8,128)S(1)}, f32[4,2,4,4,40,128]{5,4,3,2,1,0:T(8,128)S(1)}, f32[4,2,4,4,40,128]{5,4,3,2,1,0:T(8,128)S(1)}, f32[2048,128]{1,0:T(8,128)S(1)}, s32[8,128]{1,0:T(8,128)S(1)}) custom-call(f32[76,128,128]{2,1,0:T(8,128)} %flat_hbm.1, f32[1,16]{1,0:T(1,128)} %bitcast.10, s32[76,128]{1,0:T(8,128)} %bitcast.9, ...), custom_call_target="tpu_custom_call" | custom-call | tf_op jit(solution)/shard_map/exchange/pallas_call | solution.py:214
  102.0 6.4 %products.1 = (bf16[1,1536,512]{2,1,0:T(8,128)(2,1)}, bf16[1,512,7168]{2,1,0:T(8,128)(2,1)}) custom-call(s32[8,128]{1,0:T(8,128)S(1)} %get-tuple-element.7.where, f32[128,48,128]{2,1,0:T(8,128)S(1)} %bitcast.6, f32[128,40,128]{2,1,0:T(8,128)S(1)} %bitcast.7, f32[128,40,128]{2,1,0:T(8,128)S(1)} %bitcast.8, f32[2048,128]{1,0:T(8,128)S(1)} %get-tuple-element.11.gain), custom_call_target="tpu_custom_call" | custom-call | tf_op jit(solution)/shard_map/products/pallas_call | solution.py:297

commit v5 on v4

--- a/solution.py
+++ b/solution.py
@@ -166,12 +166,8 @@
 
     await_bytes(gather.at[pl.ds(0, 3), 0, :, 0], gain_sem.at[1])
     mine = gather.at[:, :, y, core]
-    for r in (1, 3, 2, 0):
-        for c in (0, 1):
-            if r or c:
-                n = 2 if r else 3
-                send(mine, mine, sent_gain.at[n], gain_sem.at[n],
-                     device(shifted(here, 2, r), (core + c) % 2))
+    for r in HOPS:
+        send(mine, mine, sent_gain.at[2], gain_sem.at[2], device(shifted(here, 2, r), core))
 
     def finish(q):
         for o in range(3):
@@ -179,10 +175,11 @@
             deliver(o, second[o].at[q - 1], q)
 
     finish(HOPS[0])
+    await_bytes(gather.at[:, :, pl.ds(0, 3), 0], gain_sem.at[2])
+    mine = gather.at[:, :, :, core]
+    send(mine, mine, sent_gain.at[3], gain_sem.at[3], device(here, 1 - core))
     finish(HOPS[1])
-    rest = gather.at[:, :, pl.ds(0, 3)]
-    await_bytes(rest, gain_sem.at[2])
-    await_bytes(gather.at[:, :, 3, 0], gain_sem.at[3])
+    await_bytes(gather.at[:, :, :, 0], gain_sem.at[3])
     turned = jnp.transpose(gather[...].reshape(HEADS, HEADS))
     for d in range(HEADS):
         gain[pl.ds(d * SHARE, SHARE)] = jnp.broadcast_to(
@@ -202,8 +199,8 @@
         await_bytes(got[o].at[0, 0], sent_core.at[o])
     await_bytes(gather.at[0, 0, pl.ds(0, 3), 0], sent_gain.at[0])
     await_bytes(gather.at[pl.ds(0, 3), 0, :, 0], sent_gain.at[1])
-    await_bytes(rest, sent_gain.at[2])
-    await_bytes(gather.at[:, :, 3, 0], sent_gain.at[3])
+    await_bytes(gather.at[:, :, pl.ds(0, 3), 0], sent_gain.at[2])
+    await_bytes(gather.at[:, :, :, 0], sent_gain.at[3])
 
 
 def exchange(flat_master, gains, place, serve_rank):
@@ -260,8 +257,6 @@
         g = gain[pl.ds(QL + b * DH, DH)]
         high, low = split(block((QL + KL) // DH + b) * g)
         uv[rows] = jnp.concatenate([high, low, high], axis=1)
-        high, low = split(jnp.transpose(block(QL // DH + b) * g))
-        uk[:, rows] = jnp.concatenate([high, high, low], axis=0)
 
     for start in range(0, D, STRIP):
         for column in range(start, start + STRIP, 2 * DH):
@@ -276,6 +271,10 @@
         strip = pl.ds(start, STRIP)
         write(vo.at[:, strip], vo_hbm.at[0, :, strip])
 
+    for b in range(KL // DH):
+        g = gain[pl.ds(QL + b * DH, DH)]
+        high, low = split(jnp.transpose(block(QL // DH + b) * g))
+        uk[:, pl.ds(b * DH, DH)] = jnp.concatenate([high, high, low], axis=0)
     for start in range(0, QL, KL):
         left = []
         for row in range(start, start + KL, DH):

time: 109 us -> 108 us (level)
  no operation moved by 1% of the time
where the time goes in v5:
time: 108 us
  Pallas kernels  107 us (99%)
    pallas_call x1, Pallas kernels, exchange(): pl.pallas_call(exchange_kernel, out_shape=parts(4, 2, 4, 4) + [pltpu.VMEM...  101 us
    pallas_call x1, Pallas kernels, products(): pl.pallas_call(product_kernel, in_specs=[pl.BlockSpec(memory_space=pltpu....  6.42 us

profile of v5, /device:TPU:1, one launch (start us, length us, event | category | flops | bytes accessed | tf_op | source)
XLA Modules:
  0.0 108.0 jit_solution(14716450530595996209)
XLA Ops:
  0.6 101.0 %exchange.1 = (f32[4,2,4,4,48,128]{5,4,3,2,1,0:T(8,128)S(1)}, f32[4,2,4,4,40,128]{5,4,3,2,1,0:T(8,128)S(1)}, f32[4,2,4,4,40,128]{5,4,3,2,1,0:T(8,128)S(1)}, f32[2048,128]{1,0:T(8,128)S(1)}, s32[8,128]{1,0:T(8,128)S(1)}) custom-call(f32[76,128,128]{2,1,0:T(8,128)} %flat_hbm.1, f32[1,16]{1,0:T(1,128)} %bitcast.10, s32[76,128]{1,0:T(8,128)} %bitcast.9, ...), custom_call_target="tpu_custom_call" | custom-call | tf_op jit(solution)/shard_map/exchange/pallas_call | solution.py:211
  101.6 6.4 %products.1 = (bf16[1,1536,512]{2,1,0:T(8,128)(2,1)}, bf16[1,512,7168]{2,1,0:T(8,128)(2,1)}) custom-call(s32[8,128]{1,0:T(8,128)S(1)} %get-tuple-element.7.where, f32[128,48,128]{2,1,0:T(8,128)S(1)} %bitcast.6, f32[128,40,128]{2,1,0:T(8,128)S(1)} %bitcast.7, f32[128,40,128]{2,1,0:T(8,128)S(1)} %bitcast.8, f32[2048,128]{1,0:T(8,128)S(1)} %get-tuple-element.11.gain), custom_call_target="tpu_custom_call" | custom-call | tf_op jit(solution)/shard_map/products/pallas_call | solution.py:296

commit v6 on v5

--- a/solution.py
+++ b/solution.py
@@ -265,8 +265,9 @@
             high = jnp.concatenate([high0, high1], axis=1)
             low = jnp.concatenate([low0, low1], axis=1)
             out = jnp.dot(
-                uv[...], jnp.concatenate([high, high, low], axis=0),
+                uv[:, pl.ds(0, 2 * DH)], jnp.concatenate([high, high], axis=0),
                 preferred_element_type=jnp.float32)
+            out += jnp.dot(uv[:, pl.ds(2 * DH, DH)], low, preferred_element_type=jnp.float32)
             vo[:, pl.ds(column, 2 * DH)] = out.astype(jnp.bfloat16)
         strip = pl.ds(start, STRIP)
         write(vo.at[:, strip], vo_hbm.at[0, :, strip])

time: 108 us -> 108 us (level)
  no operation moved by 1% of the time
where the time goes in v6:
time: 108 us
  Pallas kernels  107 us (99%)
    pallas_call x1, Pallas kernels, exchange(): pl.pallas_call(exchange_kernel, out_shape=parts(4, 2, 4, 4) + [pltpu.VMEM...  101 us
    pallas_call x1, Pallas kernels, products(): pl.pallas_call(product_kernel, in_specs=[pl.BlockSpec(memory_space=pltpu....  6.4 us

profile of v6, /device:TPU:1, one launch (start us, length us, event | category | flops | bytes accessed | tf_op | source)
XLA Modules:
  0.0 108.0 jit_solution(10908839647573085370)
XLA Ops:
  0.6 101.0 %exchange.1 = (f32[4,2,4,4,48,128]{5,4,3,2,1,0:T(8,128)S(1)}, f32[4,2,4,4,40,128]{5,4,3,2,1,0:T(8,128)S(1)}, f32[4,2,4,4,40,128]{5,4,3,2,1,0:T(8,128)S(1)}, f32[2048,128]{1,0:T(8,128)S(1)}, s32[8,128]{1,0:T(8,128)S(1)}) custom-call(f32[76,128,128]{2,1,0:T(8,128)} %flat_hbm.1, f32[1,16]{1,0:T(1,128)} %bitcast.10, s32[76,128]{1,0:T(8,128)} %bitcast.9, ...), custom_call_target="tpu_custom_call" | custom-call | tf_op jit(solution)/shard_map/exchange/pallas_call | solution.py:211
  101.6 6.4 %products.1 = (bf16[1,1536,512]{2,1,0:T(8,128)(2,1)}, bf16[1,512,7168]{2,1,0:T(8,128)(2,1)}) custom-call(s32[8,128]{1,0:T(8,128)S(1)} %get-tuple-element.7.where, f32[128,48,128]{2,1,0:T(8,128)S(1)} %bitcast.6, f32[128,40,128]{2,1,0:T(8,128)S(1)} %bitcast.7, f32[128,40,128]{2,1,0:T(8,128)S(1)} %bitcast.8, f32[2048,128]{1,0:T(8,128)S(1)} %get-tuple-element.11.gain), custom_call_target="tpu_custom_call" | custom-call | tf_op jit(solution)/shard_map/products/pallas_call | solution.py:297
